TPU v7x, 32 devices: a whole 2x2x4 slice. The times are simulated.
32 devices in a mesh: groups: 2 (over x), seq: 16 (over z, y, core).
Axes of the slice: x: 2, y: 2, z: 4, core: 2. Of those that a mesh axis runs over, the one named last changes fastest.
Arguments:
- self_query: bfloat16 [4096, 5120], P(('groups', 'seq')), parts along dimension 0, may hold values from -384 to 384
- self_key: bfloat16 [4096, 5120], P(('groups', 'seq')), parts along dimension 0, may hold values from -20 to 20
- self_value: bfloat16 [4096, 5120], P(('groups', 'seq')), parts along dimension 0, may hold values from -6 to 6
- cross_query: bfloat16 [4096, 5120], P(('groups', 'seq')), parts along dimension 0, may hold values from -384 to 384
- context: bfloat16 [512, 4096], P('groups'), parts along dimension 0, may hold values from -6 to 6
- key_weight: bfloat16 [4096, 5120], P(None, 'seq'), may hold values from -0.09375 to 0.09375
- value_weight: bfloat16 [4096, 5120], P(None, 'seq'), may hold values from -0.09375 to 0.09375
- band_width: int32 [40], replicated, may hold values from 0 to 15
Outputs:
- self_out: bfloat16 [4096, 5120], P(('groups', 'seq')), parts along dimension 0
- cross_out: bfloat16 [4096, 5120], P(('groups', 'seq')), parts along dimension 0
There are 2 independent parts, one for each index of `groups`. A program takes and returns all parts, laid end to end along the dimension named above; an argument that names none is the same for every part. Nothing has to cross between parts.
All inputs are finite; a program needn't handle non-finite values.
Results may differ from a plain program's by a relative error of at most 0.006.
The roundings to bfloat16 on the way count: a program that leaves them out, or rounds other values in their place, can miss the bound.
Values may be sent and summed in bfloat16 or wider, within the bound.
A program may use at most 128 MiB of HBM per device.

v0:
```python
import math

import jax
import jax.numpy as jnp
from jax import lax
from jax.sharding import PartitionSpec as P

SB = 16


def head_positions(band_width, stripe_ids):
    head_count = band_width.shape[0]
    head_ids = jnp.arange(head_count, dtype=jnp.int32)
    return jnp.broadcast_to(head_ids[None, :], (stripe_ids.shape[0], head_count))


def attend_task(task_data, rounds, softmax_scale):
    task_query = task_data[:, :, 0]
    task_keys = task_data[:, :, 1]
    task_values = task_data[:, :, 2]
    tok_rows, stripe_len, head_dim = task_query.shape
    scores = (
        jnp.einsum("tid,uid->tiu", task_query, task_keys, preferred_element_type=jnp.float32)
        * softmax_scale
    )
    row_max = jnp.max(scores, axis=2)
    weights = jnp.exp(scores - row_max[:, :, None])
    row_sum = jnp.sum(weights, axis=2)
    running = jnp.einsum(
        "tiu,uid->tid",
        weights.astype(jnp.bfloat16),
        task_values,
        preferred_element_type=jnp.float32,
    )
    block_ids = jnp.arange(stripe_len, dtype=jnp.int32)
    low_side = jnp.arange(2 * tok_rows, dtype=jnp.int32) < tok_rows

    def widen_band(offset, carry_in):
        row_max, row_sum, running = carry_in
        near_keys = jnp.concatenate(
            [jnp.roll(task_keys, offset, axis=1), jnp.roll(task_keys, -offset, axis=1)], axis=0
        )
        near_values = jnp.concatenate(
            [jnp.roll(task_values, offset, axis=1), jnp.roll(task_values, -offset, axis=1)], axis=0
        )
        allowed = jnp.where(
            low_side[None, :],
            (block_ids >= offset)[:, None],
            (block_ids + offset < stripe_len)[:, None],
        )
        scores = (
            jnp.einsum("tid,uid->tiu", task_query, near_keys, preferred_element_type=jnp.float32)
            * softmax_scale
        )
        scores = jnp.where(allowed[None], scores, -jnp.inf)
        new_max = jnp.maximum(row_max, jnp.max(scores, axis=2))
        rescale = jnp.exp(row_max - new_max)
        weights = jnp.where(allowed[None], jnp.exp(scores - new_max[:, :, None]), 0.0)
        row_sum = row_sum * rescale + jnp.sum(weights, axis=2)
        running = running * rescale[:, :, None] + jnp.einsum(
            "tiu,uid->tid",
            weights.astype(jnp.bfloat16),
            near_values,
            preferred_element_type=jnp.float32,
        )
        return (new_max, row_sum, running)

    row_max, row_sum, running = lax.fori_loop(
        1, jnp.maximum(rounds, 1), widen_band, (row_max, row_sum, running)
    )
    return (running / row_sum[:, :, None]).astype(jnp.bfloat16)


def shards(
    self_query, self_key, self_value, cross_query, context, key_weight, value_weight, band_width
):
    devices = lax.axis_size("seq")
    device = lax.axis_index("seq")
    tok_rows = self_query.shape[0]
    head_count = band_width.shape[0]
    head_dim = self_query.shape[1] // head_count
    softmax_scale = 1.0 / math.sqrt(head_dim)
    own_stripe = device // SB
    own_positions = head_positions(band_width, jnp.reshape(own_stripe, (1,)))[0]
    per_run = (head_count + devices - 1) // devices
    stripes_run = devices // SB
    slot_total = devices * per_run
    target = (
        own_positions + own_stripe * head_count
    ) % devices * per_run + own_positions // devices
    select = (target[None, :] == jnp.arange(slot_total, dtype=jnp.int32)[:, None]).astype(
        jnp.bfloat16
    )

    def route_heads(source):
        return jnp.einsum(
            "thd,fh->tfd",
            source.reshape(tok_rows, head_count, head_dim),
            select,
            preferred_element_type=jnp.float32,
        ).astype(jnp.bfloat16)

    outgoing = jnp.stack(
        [route_heads(self_query), route_heads(self_key), route_heads(self_value)], axis=2
    )
    arrived = lax.all_to_all(outgoing, "seq", split_axis=1, concat_axis=1, tiled=True)
    arrived = arrived.reshape(tok_rows, stripes_run, SB, per_run, 3, head_dim)
    stripe_ids = jnp.arange(stripes_run, dtype=jnp.int32)
    positions = head_positions(band_width, stripe_ids)
    slot_ids = jnp.arange(per_run, dtype=jnp.int32)
    wanted = slot_ids[None, :] * devices + (device - stripe_ids[:, None] * head_count) % devices
    matches = positions[:, None, :] == wanted[:, :, None]
    task_band = jnp.sum(jnp.where(matches, band_width[None, None, :], 0), axis=2)
    rounds = jnp.where(jnp.any(matches, axis=2), task_band + 1, 0).reshape(-1)

    def run_task(task_index, results):
        stripe_id = task_index // per_run
        slot_id = task_index % per_run
        task_data = lax.dynamic_index_in_dim(arrived, stripe_id, 1, keepdims=False)
        task_data = lax.dynamic_index_in_dim(task_data, slot_id, 2, keepdims=False)
        attended = attend_task(task_data, rounds[task_index], softmax_scale)
        return lax.dynamic_update_slice(
            results, attended[:, None, :, None, :], (0, stripe_id, 0, slot_id, 0)
        )

    results = jnp.zeros((tok_rows, stripes_run, SB, per_run, head_dim), jnp.bfloat16)
    results = lax.fori_loop(0, stripes_run * per_run, run_task, results)
    returned = lax.all_to_all(
        results.reshape(tok_rows, slot_total, head_dim),
        "seq",
        split_axis=1,
        concat_axis=1,
        tiled=True,
    )
    self_out = jnp.einsum(
        "tfd,fh->thd", returned, select, preferred_element_type=jnp.float32
    ).astype(jnp.bfloat16)
    self_out = self_out.reshape(tok_rows, head_count * head_dim)
    text_key = jnp.dot(context, key_weight, preferred_element_type=jnp.float32).astype(jnp.bfloat16)
    text_value = jnp.dot(context, value_weight, preferred_element_type=jnp.float32).astype(
        jnp.bfloat16
    )
    text_key, text_value = (
        lax.all_gather(text_key, "seq", axis=1, tiled=True),
        lax.all_gather(text_value, "seq", axis=1, tiled=True),
    )
    text_len = context.shape[0]
    scores = (
        jnp.einsum(
            "thd,uhd->thu",
            cross_query.reshape(tok_rows, head_count, head_dim),
            text_key.reshape(text_len, head_count, head_dim),
            preferred_element_type=jnp.float32,
        )
        * softmax_scale
    )
    row_max = jnp.max(scores, axis=2)
    weights = jnp.exp(scores - row_max[:, :, None])
    row_sum = jnp.sum(weights, axis=2)
    attended = jnp.einsum(
        "thu,uhd->thd",
        weights.astype(jnp.bfloat16),
        text_value.reshape(text_len, head_count, head_dim),
        preferred_element_type=jnp.float32,
    )
    cross_out = (
        (attended / row_sum[:, :, None])
        .astype(jnp.bfloat16)
        .reshape(tok_rows, head_count * head_dim)
    )
    return (self_out, cross_out)


def solution(mesh):
    in_specs = (
        P(("groups", "seq"), None),
        P(("groups", "seq"), None),
        P(("groups", "seq"), None),
        P(("groups", "seq"), None),
        P("groups", None),
        P(None, "seq"),
        P(None, "seq"),
        P(),
    )
    out_specs = (P(("groups", "seq"), None), P(("groups", "seq"), None))
    return jax.shard_map(shards, mesh=mesh, in_specs=in_specs, out_specs=out_specs, check_vma=False)
```

profile of v0, /device:TPU:18, one launch (start us, length us, event | category | flops | bytes accessed | tf_op | source)
XLA Modules:
  0.0 542.0 jit_solution(15674094273652753281)
XLA Ops:
  7.2 1.7 copy.67
  12.9 3.4 copy.48
  16.3 6.2 %all-to-all-start = ((bf16[128,48,3,128]{3,0,2,1:T(8,128)(2,1)}), bf16[128,48,3,128]{3,0,2,1:T(8,128)(2,1)}, u32[]{:S(2)}, u32[]{:S(2)}) async-start(bf16[128,48,3,128]{3,0,2,1:T(8,128)(2,1)} %copy.48), calls=%async_computation | async-start | bytes 9437184 | tf_op jit(solution)/shard_map/all_to_all | solution.py:106
  22.6 3.1 convolution_convert_fusion.4
  25.8 3.9 convolution_convert_fusion.5
  30.2 117.2 %all-to-all-done = bf16[128,48,3,128]{3,0,2,1:T(8,128)(2,1)} async-done(((bf16[128,48,3,128]{3,0,2,1:T(8,128)(2,1)}), bf16[128,48,3,128]{3,0,2,1:T(8,128)(2,1)}, u32[]{:S(2)}, u32[]{:S(2)}) %all-to-all-start) | async-done | bytes 4718624 | tf_op jit(solution)/shard_map/all_to_all | solution.py:106
  147.5 1.5 broadcast_in_dim.93.clone
  149.0 141.0 %while.60 = (s32[]{:T(128)}, bf16[128,1,16,3,128]{4,0,3,2,1:T(8,128)(2,1)}, bf16[128,1,16,3,3,128]{5,0,4,3,2,1:T(8,128)(2,1)}, s32[3]{0:T(128)S(1)}, s32[]{:T(12...) while((s32[]{:T(128)}, ...), condition=%wide.region_9.12_spmd, body=%wide.region_2.11_spmd.sunk | while | flops 416289088 | bytes 38462852 | solution.py:127
  149.0 1.5 copy_bitcast_fusion.3
  151.4 1.1 slice_bitcast_fusion.9
  152.5 1.3 copy.86
  155.2 118.4 %while.61 = (s32[]{:T(128)}, f32[128,16]{0,1:T(8,128)S(1)}, f32[128,16]{0,1:T(8,128)S(1)}, f32[128,16,128]{0,2,1:T(8,128)S(1)}, s32[]{:T(128)}, /*index=5*/bf16[...) while((s32[]{:T(128)}, f32[128,16]{0,1:T(8,128)S(1)}, ...), condition=%wide.region_8.10_spmd.clone.clone, body=%wide.region_5.9_spmd.clone.clone.sunk | while | flops 279978304 | bytes 21644316 | solution.py:68
  156.3 1.7 bitcast_reduce_fusion.3
  158.1 1.4 fusion.94
  159.8 4.5 fusion.95
  165.4 1.7 bitcast_reduce_fusion.3
  167.2 1.4 fusion.94
  168.9 4.5 fusion.95
  174.6 1.7 bitcast_reduce_fusion.3
  176.3 1.4 fusion.94
  178.0 4.5 fusion.95
  183.7 1.7 bitcast_reduce_fusion.3
  185.4 1.4 fusion.94
  187.1 4.5 fusion.95
  192.8 1.7 bitcast_reduce_fusion.3
  194.5 1.4 fusion.94
  196.2 4.5 fusion.95
  201.9 1.7 bitcast_reduce_fusion.3
  203.6 1.4 fusion.94
  205.3 4.5 fusion.95
  211.0 1.7 bitcast_reduce_fusion.3
  212.7 1.4 fusion.94
  214.4 4.5 fusion.95
  220.1 1.7 bitcast_reduce_fusion.3
  221.8 1.4 fusion.94
  223.5 4.5 fusion.95
  229.2 1.7 bitcast_reduce_fusion.3
  230.9 1.4 fusion.94
  232.6 4.5 fusion.95
  238.3 1.7 bitcast_reduce_fusion.3
  240.1 1.4 fusion.94
  241.8 4.5 fusion.95
  247.4 1.7 bitcast_reduce_fusion.3
  249.2 1.4 fusion.94
  250.9 4.5 fusion.95
  256.5 1.7 bitcast_reduce_fusion.3
  258.3 1.4 fusion.94
  260.0 4.5 fusion.95
  265.6 1.7 bitcast_reduce_fusion.3
  267.4 1.4 fusion.94
  269.1 4.5 fusion.95
  274.9 1.5 copy_bitcast_fusion.3
  278.4 1.3 copy.86
  282.5 1.5 copy_bitcast_fusion.3
  284.9 1.1 slice_bitcast_fusion.9
  286.0 1.3 copy.86
  290.0 204.4 %all-to-all-start.1 = ((bf16[128,48,128]{2,0,1:T(8,128)(2,1)}), bf16[128,48,128]{2,0,1:T(8,128)(2,1)}, u32[]{:S(2)}, u32[]{:S(2)}) async-start(bf16[128,48,128]{2,0,1:T(8,128)(2,1)} %bitcast.135), calls=%async_computation.1 | async-start | bytes 3145728 | tf_op jit(solution)/shard_map/all_to_all | solution.py:128
  494.4 5.1 bitcast_reduce_fusion.1
  499.6 3.4 fusion.36
  503.0 5.8 %fusion.40 = bf16[128,40,128]{0,2,1:T(8,128)(2,1)} fusion(f32[128,40]{0,1:T(8,128)S(1)} %fusion.36, bf16[256,40,128]{0,2,1:T(8,128)(2,1)} %bitcast.146, f32[40,256,128]{2,1,0:T(8,128)} %get-tuple-element.314, f32[128,40]{0,1:T(8,128)S(1)} %get-tuple-element.313), kind=kOutput, calls=%fused_computation.67 | convolution fusion | flops 340787200 | bytes 9216000 | tf_op jit(solution)/shard_map/thu,uhd->thd/dot_general | solution.py:160
  508.9 2.6 copy.56
  511.4 19.8 %all-to-all-done.1 = bf16[128,48,128]{2,0,1:T(8,128)(2,1)} async-done(((bf16[128,48,128]{2,0,1:T(8,128)(2,1)}), bf16[128,48,128]{2,0,1:T(8,128)(2,1)}, u32[]{:S(2)}, u32[]{:S(2)}) %all-to-all-start.1) | async-done | bytes 1572896 | tf_op jit(solution)/shard_map/all_to_all | solution.py:128
  531.2 2.7 convolution_convert_fusion.3
  533.9 1.3 copy.81
  (239 shorter events, 30.4 us)
Async XLA Ops:
  7.2 15.4 %copy-start = (bf16[4096,320]{0,1:T(8,128)(2,1)S(1)}, bf16[4096,320]{0,1:T(8,128)(2,1)}, u32[]{:S(2)}) copy-start(bf16[4096,320]{0,1:T(8,128)(2,1)} %param.21) | copy-start | bytes 7864324
  7.2 1.9 copy-start.3
  7.2 4.4 copy-start.6
  10.0 1.3 copy-start.4
  16.3 131.1 %all-to-all-start = ((bf16[128,48,3,128]{3,0,2,1:T(8,128)(2,1)}), bf16[128,48,3,128]{3,0,2,1:T(8,128)(2,1)}, u32[]{:S(2)}, u32[]{:S(2)}) async-start(bf16[128,48,3,128]{3,0,2,1:T(8,128)(2,1)} %copy.48), calls=%async_computation | async-start | bytes 9437184 | tf_op jit(solution)/shard_map/all_to_all | solution.py:106
  22.5 471.9 %all-gather.5.cloned.1.call-start = ((), (), s32[]{:S(2)}) async-start(), calls=%async_computation.3 | async-start | bytes 2785280 | tf_op jit(solution)/shard_map/all_gather | solution.py:144
  25.7 4.3 copy-start.8
  25.7 477.3 %all-gather.3.cloned.1.call-start = ((), (), s32[]{:S(2)}) async-start(), calls=%async_computation.2 | async-start | bytes 2785280 | tf_op jit(solution)/shard_map/all_gather | solution.py:145
  155.3 1.0 copy-start.2
  164.4 1.0 copy-start.2
  173.5 1.0 copy-start.2
  182.6 1.0 copy-start.2
  191.7 1.0 copy-start.2
  200.8 1.0 copy-start.2
  209.9 1.0 copy-start.2
  219.1 1.0 copy-start.2
  228.2 1.0 copy-start.2
  237.3 1.0 copy-start.2
  246.4 1.0 copy-start.2
  255.5 1.0 copy-start.2
  264.6 1.0 copy-start.2
  290.0 204.4 %copy-start.5 = (bf16[128,5120]{1,0:T(8,128)(2,1)S(1)}, bf16[128,5120]{1,0:T(8,128)(2,1)}, u32[]{:S(2)}) copy-start(bf16[128,5120]{1,0:T(8,128)(2,1)} %param.19) | copy-start | bytes 3932164
  290.0 241.2 %all-to-all-start.1 = ((bf16[128,48,128]{2,0,1:T(8,128)(2,1)}), bf16[128,48,128]{2,0,1:T(8,128)(2,1)}, u32[]{:S(2)}, u32[]{:S(2)}) async-start(bf16[128,48,128]{2,0,1:T(8,128)(2,1)} %bitcast.135), calls=%async_computation.1 | async-start | bytes 3145728 | tf_op jit(solution)/shard_map/all_to_all | solution.py:128
  508.9 22.4 %copy-start.7 = (s32[40]{0:T(128)S(1)}, s32[40]{0:T(128)}, u32[]{:S(2)}) copy-start(s32[40]{0:T(128)} %copy-done.6) | copy-start | bytes 484
  508.9 26.3 %copy-start.1 = (bf16[4096,320]{0,1:T(8,128)(2,1)S(1)}, bf16[4096,320]{0,1:T(8,128)(2,1)}, u32[]{:S(2)}) copy-start(bf16[4096,320]{0,1:T(8,128)(2,1)} %param.21) | copy-start | bytes 7864324
Sparse Core Ops, SparseCore 0:
  25.8 97.1 all-gather.4
  125.3 44.0 all-gather.2
where the time goes:
time: 552 us; the launch traced here: 542 us
  starting transfers between devices  211 us (38%)
  waiting for transfers between devices  137 us (25%)
  matrix products  107 us (19%)
  local copies, waits for them, and re-layouts  43.6 us (8%)
  other arithmetic  25.3 us (5%)
  between operations  14.2 us (3%)
    all_to_all x1, starting transfers between devices, shards(): lax.all_to_all(results.reshape(tok_rows, slot_total, head_dim), 'seq', sp...  204 us
    all_to_all x1, waiting for transfers between devices, shards(): lax.all_to_all(outgoing, 'seq', split_axis=1, concat_axis=1, tiled=True)  117 us
    dot_general x13, matrix products, widen_band(): jnp.einsum('tiu,uid->tid', weights.astype(jnp.bfloat16), near_values, pre...  59.1 us
    dot_general x13, matrix products, widen_band(): jnp.einsum('tid,uid->tiu', task_query, near_keys, preferred_element_type=...  22.4 us
    all_to_all x1, waiting for transfers between devices, shards(): lax.all_to_all(results.reshape(tok_rows, slot_total, head_dim), 'seq', sp...  19.8 us
    reduce_sum x13, other arithmetic, widen_band(): row_sum = row_sum * rescale + jnp.sum(weights, axis=2)  18.6 us
    while x68, local copies, waits for them, and re-layouts  14.5 us
  transfers between devices with their start and end apart: 4, of which 2 were waited for; matrix products, arithmetic and copies ran while one was open for 28% of the time, Pallas kernels for 0%

commit v1 on v0

v1 whole, which is shorter than its diff:
```python
import functools
import math

import jax
import jax.numpy as jnp
from jax import lax
from jax.experimental import pallas as pl
from jax.experimental.pallas import tpu as pltpu
from jax.sharding import PartitionSpec as P

SB = 16
PLANE = 4
NT = (((1,), (1,)), ((), ()))
MESH = pl.DeviceIdType.MESH


def kernel(
    devices,
    scale,
    band_ref,
    query_ref,
    key_ref,
    value_ref,
    cross_ref,
    context_ref,
    key_weight_ref,
    value_weight_ref,
    self_out_ref,
    cross_out_ref,
    held,
    attended,
    text,
    context_buf,
    weight_buf,
    load_sem,
    send_sem,
    edge_sem,
    recv_sem,
    back_send_sem,
    back_recv_sem,
    text_send_sem,
    text_recv_sem,
):
    heads = band_ref.shape[0]
    rows = query_ref.shape[0]
    dim = query_ref.shape[1] // heads
    text_cols = key_weight_ref.shape[1]
    device = lax.axis_index("seq")
    me = device % SB
    stripe = device - me
    full = heads // SB
    rest = heads - full * SB
    stride = SB // rest if rest else 1
    sources = (query_ref, key_ref, value_ref)

    def head_cols(head):
        return pl.ds(pl.multiple_of(head * dim, dim), dim)

    def block_rows(index):
        return pl.ds(pl.multiple_of(index * rows, rows), rows)

    loads = [
        pltpu.make_async_copy(source, target, load_sem.at[index])
        for index, (source, target) in enumerate(
            (
                (context_ref, context_buf),
                (key_weight_ref, weight_buf.at[0]),
                (value_weight_ref, weight_buf.at[1]),
            )
        )
    ]
    for load in loads:
        load.start()

    plane = device // PLANE
    place = device % PLANE
    planes = devices // PLANE
    across = plane * PLANE + (1 - place // 2) * 2 + place % 2
    beside = plane * PLANE + (place // 2) * 2 + (1 - place % 2)

    barrier = pltpu.get_barrier_semaphore()

    def greet(step, carry):
        peer = stripe + (me + step) % SB
        pl.semaphore_signal(barrier, inc=1, device_id={"seq": peer}, device_id_type=MESH)
        return carry

    lax.fori_loop(1, SB, greet, 0)

    def greet_plane(step, carry):
        peer_plane = (plane + step) % planes

        @pl.when(peer_plane // (SB // PLANE) != device // SB)
        def _():
            peer = peer_plane * PLANE + place
            pl.semaphore_signal(barrier, inc=1, device_id={"seq": peer}, device_id_type=MESH)

        return carry

    lax.fori_loop(1, planes, greet_plane, 0)
    pl.semaphore_wait(barrier, SB - 1 + planes - SB // PLANE)

    def send_head(slot, head, peer, sem):
        for index, source in enumerate(sources):
            pltpu.make_async_remote_copy(
                src_ref=source.at[:, head_cols(head)],
                dst_ref=held.at[slot, index, block_rows(me), :],
                send_sem=sem,
                recv_sem=recv_sem.at[slot],
                device_id={"seq": stripe + peer},
                device_id_type=MESH,
            ).start()

    def keep_head(slot, head):
        for index, source in enumerate(sources):
            pltpu.make_async_copy(
                source.at[:, head_cols(head)],
                held.at[slot, index, block_rows(me), :],
                recv_sem.at[slot],
            ).start()

    for slot in range(full):

        def send_full(step, carry, slot=slot):
            peer = (me + step) % SB
            send_head(slot, slot * SB + peer, peer, send_sem.at[slot])
            return carry

        lax.fori_loop(1, SB, send_full, 0)
        keep_head(slot, slot * SB + me)

        if slot == 0:
            for load in loads:
                load.wait()
            for index in range(2):
                depth = context_buf.shape[1] // 8

                def project(step, total, index=index, depth=depth):
                    part = pl.ds(pl.multiple_of(step * depth, depth), depth)
                    return total + jnp.dot(
                        context_buf[:, part],
                        weight_buf[index, part, :],
                        preferred_element_type=jnp.float32,
                    )

                total = lax.fori_loop(
                    0, 8, project, jnp.zeros((context_buf.shape[0], text_cols), jnp.float32)
                )
                own = pl.ds(pl.multiple_of(device * text_cols, text_cols), text_cols)
                text[index, own, :] = total.T.astype(jnp.bfloat16)

            def send_text(step, carry):
                peer = ((plane + step) % planes) * PLANE + place
                piece = pl.ds(pl.multiple_of(device * text_cols, text_cols), text_cols)
                pltpu.make_async_remote_copy(
                    src_ref=text.at[:, piece, :],
                    dst_ref=text.at[:, piece, :],
                    send_sem=text_send_sem.at[0],
                    recv_sem=text_recv_sem.at[0],
                    device_id={"seq": peer},
                    device_id_type=MESH,
                ).start()
                return carry

            lax.fori_loop(1, planes, send_text, 0)

    if rest:
        mine = (me % stride == 0) & (me // stride < rest)
        base = me // stride

        def send_rest(step, carry):
            index = (base + step) % rest
            send_head(full, full * SB + index, index * stride, send_sem.at[full])
            return carry

        lax.fori_loop(1, rest, send_rest, 0)
        first = base % rest

        @pl.when(mine)
        def _():
            keep_head(full, full * SB + first)

        @pl.when(jnp.logical_not(mine))
        def _():
            send_head(full, full * SB + first, first * stride, edge_sem)

    def forward_text(phase, peer, places):
        for at in places:

            def forward(step, carry, at=at):
                owner = step * PLANE + at
                piece = pl.ds(pl.multiple_of(owner * text_cols, text_cols), text_cols)
                pltpu.make_async_remote_copy(
                    src_ref=text.at[:, piece, :],
                    dst_ref=text.at[:, piece, :],
                    send_sem=text_send_sem.at[phase],
                    recv_sem=text_recv_sem.at[phase],
                    device_id={"seq": peer},
                    device_id_type=MESH,
                ).start()
                return carry

            lax.fori_loop(0, planes, forward, 0)

    def wait_text(sem, count):
        whole = text.at[:, pl.ds(0, count * text_cols), :]
        pltpu.make_async_copy(whole, whole, sem).wait()

    stripe_len = held.shape[2]
    tile = 2 * rows

    def attend(slot, head):
        band = band_ref[head]
        block_ids = lax.broadcasted_iota(jnp.int32, (1, stripe_len), 1) // rows

        def attend_tile(step, carry):
            at = pl.ds(pl.multiple_of(step * tile, tile), tile)
            scores = lax.dot_general(
                held[slot, 0, at, :], held[slot, 1], NT, preferred_element_type=jnp.float32
            )
            for half in range(2):
                gap = jnp.abs(block_ids - (2 * step + half))
                mask = jnp.where(gap <= band, 0.0, -jnp.inf)
                part = scores[half * rows : (half + 1) * rows] + mask
                top = jnp.max(part, axis=1, keepdims=True)
                weights = jnp.exp2((part - top) * (scale * math.log2(math.e)))
                total = jnp.sum(weights, axis=1, keepdims=True)
                summed = jnp.dot(
                    weights.astype(jnp.bfloat16),
                    held[slot, 2],
                    preferred_element_type=jnp.float32,
                )
                attended[slot, block_rows(2 * step + half), :] = (summed / total).astype(
                    jnp.bfloat16
                )
            return carry

        lax.fori_loop(0, stripe_len // tile, attend_tile, 0)

    def give_back(slot, head):
        def give(step, carry):
            peer = (me + step) % SB
            pltpu.make_async_remote_copy(
                src_ref=attended.at[slot, block_rows(peer), :],
                dst_ref=self_out_ref.at[:, head_cols(head)],
                send_sem=back_send_sem.at[slot],
                recv_sem=back_recv_sem,
                device_id={"seq": stripe + peer},
                device_id_type=MESH,
            ).start()
            return carry

        lax.fori_loop(1, SB, give, 0)
        pltpu.make_async_copy(
            attended.at[slot, block_rows(me), :],
            self_out_ref.at[:, head_cols(head)],
            back_recv_sem,
        ).start()

    def wait_held(slot):
        pltpu.make_async_copy(held.at[slot], held.at[slot], recv_sem.at[slot]).wait()

    def cross():
        def cross_head(head, carry):
            at = pl.ds(pl.multiple_of(head * dim, dim), dim)
            scores = jnp.dot(
                cross_ref[:, at], text[0, at, :], preferred_element_type=jnp.float32
            )
            top = jnp.max(scores, axis=1, keepdims=True)
            weights = jnp.exp2((scores - top) * (scale * math.log2(math.e)))
            total = jnp.sum(weights, axis=1, keepdims=True)
            summed = lax.dot_general(
                weights.astype(jnp.bfloat16), text[1, at, :], NT, preferred_element_type=jnp.float32
            )
            cross_out_ref[:, at] = (summed / total).astype(jnp.bfloat16)
            return carry

        lax.fori_loop(0, heads, cross_head, 0, unroll=4 if heads % 4 == 0 else 1)

    wait_text(text_recv_sem.at[0], planes - 1)
    forward_text(1, across, (place,))
    wait_held(0)
    attend(0, me)
    give_back(0, me)
    wait_text(text_recv_sem.at[1], planes)
    forward_text(2, beside, (place, (1 - place // 2) * 2 + place % 2))
    for slot in range(1, full):
        wait_held(slot)
        attend(slot, slot * SB + me)
        give_back(slot, slot * SB + me)
    wait_text(text_recv_sem.at[2], 2 * planes)
    cross()
    if rest:

        @pl.when(mine)
        def _():
            wait_held(full)
            attend(full, full * SB + first)
            give_back(full, full * SB + first)
            done = attended.at[full, pl.ds(0, (SB - 1) * rows), :]
            pltpu.make_async_copy(done, done, back_send_sem.at[full]).wait()

        @pl.when(jnp.logical_not(mine))
        def _():
            sent = held.at[full, :, pl.ds(0, rows), :]
            pltpu.make_async_copy(sent, sent, edge_sem).wait()

        sent = held.at[full, :, pl.ds(0, (rest - 1) * rows), :]
        pltpu.make_async_copy(sent, sent, send_sem.at[full]).wait()

    for slot in range(full):
        sent = held.at[slot, :, pl.ds(0, (SB - 1) * rows), :]
        pltpu.make_async_copy(sent, sent, send_sem.at[slot]).wait()
        done = attended.at[slot, pl.ds(0, (SB - 1) * rows), :]
        pltpu.make_async_copy(done, done, back_send_sem.at[slot]).wait()
    wait_text(text_send_sem.at[0], planes - 1)
    wait_text(text_send_sem.at[1], planes)
    wait_text(text_send_sem.at[2], 2 * planes)
    pltpu.make_async_copy(self_out_ref, self_out_ref, back_recv_sem).wait()


def shards(
    self_query, self_key, self_value, cross_query, context, key_weight, value_weight, band_width
):
    devices = lax.axis_size("seq")
    rows, width = self_query.shape
    heads = band_width.shape[0]
    dim = width // heads
    slots = (heads + SB - 1) // SB
    text_len, depth = context.shape
    text_cols = key_weight.shape[1]
    vmem = pl.BlockSpec(memory_space=pltpu.VMEM)
    hbm = pl.BlockSpec(memory_space=pl.ANY)
    dtype = jnp.bfloat16
    return pl.pallas_call(
        functools.partial(kernel, devices, 1.0 / math.sqrt(dim)),
        out_shape=(
            jax.ShapeDtypeStruct((rows, width), dtype),
            jax.ShapeDtypeStruct((rows, width), dtype),
        ),
        in_specs=[
            pl.BlockSpec(memory_space=pltpu.SMEM),
            hbm,
            hbm,
            hbm,
            vmem,
            hbm,
            hbm,
            hbm,
        ],
        out_specs=(vmem, vmem),
        scratch_shapes=[
            pltpu.VMEM((slots, 3, SB * rows, dim), dtype),
            pltpu.VMEM((slots, SB * rows, dim), dtype),
            pltpu.VMEM((2, width, text_len), dtype),
            pltpu.VMEM((text_len, depth), dtype),
            pltpu.VMEM((2, depth, text_cols), dtype),
            pltpu.SemaphoreType.DMA((3,)),
            pltpu.SemaphoreType.DMA((slots,)),
            pltpu.SemaphoreType.DMA,
            pltpu.SemaphoreType.DMA((slots,)),
            pltpu.SemaphoreType.DMA((slots,)),
            pltpu.SemaphoreType.DMA,
            pltpu.SemaphoreType.DMA((3,)),
            pltpu.SemaphoreType.DMA((3,)),
        ],
        compiler_params=pltpu.CompilerParams(
            collective_id=0, has_side_effects=True, vmem_limit_bytes=56 * 1024 * 1024
        ),
        cost_estimate=pl.CostEstimate(
            flops=4 * slots * (SB * rows) ** 2 * dim,
            bytes_accessed=16 * rows * width,
            transcendentals=slots * (SB * rows) ** 2,
        ),
    )(
        band_width,
        self_query,
        self_key,
        self_value,
        cross_query,
        context,
        key_weight,
        value_weight,
    )


def solution(mesh):
    in_specs = (
        P(("groups", "seq"), None),
        P(("groups", "seq"), None),
        P(("groups", "seq"), None),
        P(("groups", "seq"), None),
        P("groups", None),
        P(None, "seq"),
        P(None, "seq"),
        P(),
    )
    out_specs = (P(("groups", "seq"), None), P(("groups", "seq"), None))
    return jax.shard_map(shards, mesh=mesh, in_specs=in_specs, out_specs=out_specs, check_vma=False)
```

time: 552 us -> 179 us (0.32); the launches traced: 542 us -> 178 us
  starting transfers between devices: 211 us -> 0 us
  Pallas kernels: 0 us -> 166 us
  waiting for transfers between devices: 137 us -> 0 us
  matrix products: 107 us -> 0 us
  local copies, waits for them, and re-layouts: 43.6 us -> 11.1 us
  other arithmetic: 25.3 us -> 0 us
  between operations: 14.2 us -> 0.66 us
    all_to_all x2 -> x0, starting transfers between devices: 211 us -> none  [the longest x1 204 us: shards(): lax.all_to_all(results.reshape(tok_rows, slot_total, head_dim), 'seq', sp...]
    pallas_call x0 -> x1, Pallas kernels: none -> 166 us  [shards(): pl.pallas_call(functools.partial(kernel, devices, 1.0 / math.sqrt(dim)),...]
    all_to_all x2 -> x0, waiting for transfers between devices: 137 us -> none  [the longest x1 117 us: shards(): lax.all_to_all(outgoing, 'seq', split_axis=1, concat_axis=1, tiled=True)]
    dot_general x40 -> x0, matrix products: 107 us -> none  [the longest x13 59.1 us: widen_band(): jnp.einsum('tiu,uid->tid', weights.astype(jnp.bfloat16), near_values, pre...]
    reduce_sum x18 -> x0, other arithmetic: 22.7 us -> none  [the longest x13 18.6 us: widen_band(): row_sum = row_sum * rescale + jnp.sum(weights, axis=2)]
    while x68 -> x0, local copies, waits for them, and re-layouts: 14.5 us -> none
    squeeze x6 -> x0, local copies, waits for them, and re-layouts: 7.81 us -> none  [the longest x3 4.53 us: run_task(): task_data = lax.dynamic_index_in_dim(task_data, slot_id, 2, keepdims=False)]
    unnamed x21 -> x8, local copies, waits for them, and re-layouts: 6.88 us -> 11.1 us
  transfers between devices with their start and end apart: 4 -> 0, of which waited for: 2 -> 0; matrix products, arithmetic and copies ran while one was open for 28% -> 0% of each run, Pallas kernels for 0% -> 0%
where the time goes in v1:
time: 179 us; the launch traced here: 178 us
  Pallas kernels  166 us (93%)
  local copies, waits for them, and re-layouts  11.1 us (6%)
    pallas_call x1, Pallas kernels, shards(): pl.pallas_call(functools.partial(kernel, devices, 1.0 / math.sqrt(dim)),...  166 us
    unnamed x8, local copies, waits for them, and re-layouts  11.1 us

profile of v1, /device:TPU:18, one launch (start us, length us, event | category | flops | bytes accessed | tf_op | source)
XLA Modules:
  0.0 177.6 jit_solution(6351918440110346437)
XLA Ops:
  0.6 0.0 copy-start
  0.6 4.7 %copy.10.key_weight_ref = bf16[4096,320]{1,0:T(8,128)(2,1)} copy(bf16[4096,320]{0,1:T(8,128)(2,1)} %param.13) | data formatting | bytes 5242880 | tf_op args[5]
  5.4 0.0 copy-done
  5.4 2.8 %copy.11.value_weight_ref = bf16[4096,320]{1,0:T(8,128)(2,1)} copy(bf16[4096,320]{0,1:T(8,128)(2,1)S(1)} %copy-done) | data formatting | bytes 5242880 | tf_op args[6]
  8.1 165.8 %shard_map.95 = (bf16[128,5120]{1,0:T(8,128)(2,1)}, bf16[128,5120]{1,0:T(8,128)(2,1)}) custom-call(s32[40]{0:T(128)} %band_ref.1, bf16[128,5120]{1,0:T(8,128)(2,1)} %query_ref.1, bf16[128,5120]{1,0:T(8,128)(2,1)} %key_ref.1, bf16[128,5120]{1,0:T(8,128)(2,1)} %value_ref.1, bf16[128,5120]{1,0:T(8,128)(2,1)} %cross_ref.1, bf16[256,4096]{1,0:T(8,128)(2,1)} %context_ref.1, ...), custom_call_target="tpu_custom_call" | custom-call | flops 6442450944 | bytes 10485760 | tf_op jit(solution)/shard_map/pallas_call | solution.py:335
  174.0 0.0 copy-start.1
  174.0 2.6 %copy.14 = bf16[128,5120]{1,0:T(8,128)(2,1)} copy(bf16[128,5120]{1,0:T(8,128)(2,1)} %get-tuple-element.4) | data formatting | bytes 2621440
  176.6 0.0 copy-done.1
  176.6 1.1 copy.15
Async XLA Ops:
  0.6 4.7 %copy-start = (bf16[4096,320]{0,1:T(8,128)(2,1)S(1)}, bf16[4096,320]{0,1:T(8,128)(2,1)}, u32[]{:S(2)}) copy-start(bf16[4096,320]{0,1:T(8,128)(2,1)} %param.14) | copy-start | bytes 7864324
  174.0 2.6 %copy-start.1 = (bf16[128,5120]{1,0:T(8,128)(2,1)S(1)}, bf16[128,5120]{1,0:T(8,128)(2,1)}, u32[]{:S(2)}) copy-start(bf16[128,5120]{1,0:T(8,128)(2,1)} %get-tuple-element.5) | copy-start | bytes 3932164

commit v2 on v1

--- a/solution.py
+++ b/solution.py
@@ -40,11 +40,13 @@
     back_recv_sem,
     text_send_sem,
     text_recv_sem,
+    pass_send_sem,
+    pass_recv_sem,
 ):
     heads = band_ref.shape[0]
     rows = query_ref.shape[0]
     dim = query_ref.shape[1] // heads
-    text_cols = key_weight_ref.shape[1]
+    text_cols = key_weight_ref.shape[0]
     device = lax.axis_index("seq")
     me = device % SB
     stripe = device - me
@@ -87,18 +89,20 @@
 
     lax.fori_loop(1, SB, greet, 0)
 
-    def greet_plane(step, carry):
-        peer_plane = (plane + step) % planes
-
-        @pl.when(peer_plane // (SB // PLANE) != device // SB)
-        def _():
-            peer = peer_plane * PLANE + place
+    pl.semaphore_wait(barrier, SB - 1)
+    for side in (-1, 1):
+        next_plane = plane + side
+
+        @pl.when(
+            (next_plane >= 0)
+            & (next_plane < planes)
+            & ((next_plane + planes) // (SB // PLANE) != (plane + planes) // (SB // PLANE))
+        )
+        def _(next_plane=next_plane):
+            peer = next_plane * PLANE + place
             pl.semaphore_signal(barrier, inc=1, device_id={"seq": peer}, device_id_type=MESH)
-
-        return carry
-
-    lax.fori_loop(1, planes, greet_plane, 0)
-    pl.semaphore_wait(barrier, SB - 1 + planes - SB // PLANE)
+            pl.semaphore_wait(barrier, 1)
+
 
     def send_head(slot, head, peer, sem):
         for index, source in enumerate(sources):
@@ -119,50 +123,78 @@
                 recv_sem.at[slot],
             ).start()
 
-    for slot in range(full):
-
-        def send_full(step, carry, slot=slot):
+    def send_full(slot, low, high):
+        def send(step, carry):
             peer = (me + step) % SB
             send_head(slot, slot * SB + peer, peer, send_sem.at[slot])
             return carry
 
-        lax.fori_loop(1, SB, send_full, 0)
+        lax.fori_loop(low, high, send, 0)
+
+    def text_piece(owner):
+        return text.at[:, pl.ds(pl.multiple_of(owner * text_cols, text_cols), text_cols), :]
+
+    def pass_text(hop, side, act):
+        come_from = plane - side * hop
+        go_to = plane + side
+
+        @pl.when((come_from >= 0) & (come_from < planes) & (go_to >= 0) & (go_to < planes))
+        def _():
+            piece = text_piece(come_from * PLANE + place)
+            way = (side + 1) // 2
+            copy = pltpu.make_async_remote_copy(
+                src_ref=piece,
+                dst_ref=piece,
+                send_sem=pass_send_sem.at[way, hop],
+                recv_sem=pass_recv_sem.at[way, hop],
+                device_id={"seq": go_to * PLANE + place},
+                device_id_type=MESH,
+            )
+            if act == "start":
+                copy.start()
+            else:
+                copy.wait_send()
+
+    def take_text(hop, side):
+        come_from = plane - side * (hop + 1)
+
+        @pl.when((come_from >= 0) & (come_from < planes))
+        def _():
+            piece = text_piece(come_from * PLANE + place)
+            pltpu.make_async_copy(piece, piece, pass_recv_sem.at[(side + 1) // 2, hop]).wait()
+
+    cuts = [1 + (SB - 1) * part // planes for part in range(planes + 1)]
+    send_full(0, cuts[0], cuts[1])
+    keep_head(0, me)
+    for load in loads:
+        load.wait()
+    for index in range(2):
+        depth = context_buf.shape[1] // 8
+
+        def project(step, total, index=index, depth=depth):
+            part = pl.ds(pl.multiple_of(step * depth, depth), depth)
+            return total + lax.dot_general(
+                weight_buf[index, :, part],
+                context_buf[:, part],
+                NT,
+                preferred_element_type=jnp.float32,
+            )
+
+        total = lax.fori_loop(
+            0, 8, project, jnp.zeros((text_cols, context_buf.shape[0]), jnp.float32)
+        )
+        own = pl.ds(pl.multiple_of(device * text_cols, text_cols), text_cols)
+        text[index, own, :] = total.astype(jnp.bfloat16)
+    for hop in range(planes - 1):
+        if hop:
+            for side in (-1, 1):
+                take_text(hop - 1, side)
+        for side in (-1, 1):
+            pass_text(hop, side, "start")
+        send_full(0, cuts[hop + 1], cuts[hop + 2])
+    for slot in range(1, full):
+        send_full(slot, 1, SB)
         keep_head(slot, slot * SB + me)
-
-        if slot == 0:
-            for load in loads:
-                load.wait()
-            for index in range(2):
-                depth = context_buf.shape[1] // 8
-
-                def project(step, total, index=index, depth=depth):
-                    part = pl.ds(pl.multiple_of(step * depth, depth), depth)
-                    return total + jnp.dot(
-                        context_buf[:, part],
-                        weight_buf[index, part, :],
-                        preferred_element_type=jnp.float32,
-                    )
-
-                total = lax.fori_loop(
-                    0, 8, project, jnp.zeros((context_buf.shape[0], text_cols), jnp.float32)
-                )
-                own = pl.ds(pl.multiple_of(device * text_cols, text_cols), text_cols)
-                text[index, own, :] = total.T.astype(jnp.bfloat16)
-
-            def send_text(step, carry):
-                peer = ((plane + step) % planes) * PLANE + place
-                piece = pl.ds(pl.multiple_of(device * text_cols, text_cols), text_cols)
-                pltpu.make_async_remote_copy(
-                    src_ref=text.at[:, piece, :],
-                    dst_ref=text.at[:, piece, :],
-                    send_sem=text_send_sem.at[0],
-                    recv_sem=text_recv_sem.at[0],
-                    device_id={"seq": peer},
-                    device_id_type=MESH,
-                ).start()
-                return carry
-
-            lax.fori_loop(1, planes, send_text, 0)
 
     if rest:
         mine = (me % stride == 0) & (me // stride < rest)
@@ -188,11 +220,10 @@
         for at in places:
 
             def forward(step, carry, at=at):
-                owner = step * PLANE + at
-                piece = pl.ds(pl.multiple_of(owner * text_cols, text_cols), text_cols)
+                piece = text_piece(step * PLANE + at)
                 pltpu.make_async_remote_copy(
-                    src_ref=text.at[:, piece, :],
-                    dst_ref=text.at[:, piece, :],
+                    src_ref=piece,
+                    dst_ref=piece,
                     send_sem=text_send_sem.at[phase],
                     recv_sem=text_recv_sem.at[phase],
                     device_id={"seq": peer},
@@ -277,18 +308,19 @@
 
         lax.fori_loop(0, heads, cross_head, 0, unroll=4 if heads % 4 == 0 else 1)
 
-    wait_text(text_recv_sem.at[0], planes - 1)
-    forward_text(1, across, (place,))
+    for side in (-1, 1):
+        take_text(planes - 2, side)
+    forward_text(0, across, (place,))
     wait_held(0)
     attend(0, me)
     give_back(0, me)
-    wait_text(text_recv_sem.at[1], planes)
-    forward_text(2, beside, (place, (1 - place // 2) * 2 + place % 2))
+    wait_text(text_recv_sem.at[0], planes)
+    forward_text(1, beside, (place, (1 - place // 2) * 2 + place % 2))
     for slot in range(1, full):
         wait_held(slot)
         attend(slot, slot * SB + me)
         give_back(slot, slot * SB + me)
-    wait_text(text_recv_sem.at[2], 2 * planes)
+    wait_text(text_recv_sem.at[1], 2 * planes)
     cross()
     if rest:
 
@@ -313,9 +345,11 @@
         pltpu.make_async_copy(sent, sent, send_sem.at[slot]).wait()
         done = attended.at[slot, pl.ds(0, (SB - 1) * rows), :]
         pltpu.make_async_copy(done, done, back_send_sem.at[slot]).wait()
-    wait_text(text_send_sem.at[0], planes - 1)
-    wait_text(text_send_sem.at[1], planes)
-    wait_text(text_send_sem.at[2], 2 * planes)
+    for hop in range(planes - 1):
+        for side in (-1, 1):
+            pass_text(hop, side, "wait")
+    wait_text(text_send_sem.at[0], planes)
+    wait_text(text_send_sem.at[1], 2 * planes)
     pltpu.make_async_copy(self_out_ref, self_out_ref, back_recv_sem).wait()
 
 
@@ -354,15 +388,17 @@
             pltpu.VMEM((slots, SB * rows, dim), dtype),
             pltpu.VMEM((2, width, text_len), dtype),
             pltpu.VMEM((text_len, depth), dtype),
-            pltpu.VMEM((2, depth, text_cols), dtype),
+            pltpu.VMEM((2, text_cols, depth), dtype),
             pltpu.SemaphoreType.DMA((3,)),
             pltpu.SemaphoreType.DMA((slots,)),
             pltpu.SemaphoreType.DMA,
             pltpu.SemaphoreType.DMA((slots,)),
             pltpu.SemaphoreType.DMA((slots,)),
             pltpu.SemaphoreType.DMA,
-            pltpu.SemaphoreType.DMA((3,)),
-            pltpu.SemaphoreType.DMA((3,)),
+            pltpu.SemaphoreType.DMA((2,)),
+            pltpu.SemaphoreType.DMA((2,)),
+            pltpu.SemaphoreType.DMA((2, devices // PLANE)),
+            pltpu.SemaphoreType.DMA((2, devices // PLANE)),
         ],
         compiler_params=pltpu.CompilerParams(
             collective_id=0, has_side_effects=True, vmem_limit_bytes=56 * 1024 * 1024
@@ -379,8 +415,8 @@
         self_value,
         cross_query,
         context,
-        key_weight,
-        value_weight,
+        key_weight.T,
+        value_weight.T,
     )
 
 

time: 179 us -> 168 us (0.939)
  local copies, waits for them, and re-layouts: 11.1 us -> 3.62 us
  Pallas kernels: 166 us -> 162 us
    unnamed x8 -> x4, local copies, waits for them, and re-layouts: 11.1 us -> 3.62 us
    pallas_call x1, Pallas kernels: 166 us -> 162 us  [shards(): pl.pallas_call(functools.partial(kernel, devices, 1.0 / math.sqrt(dim)),...]
where the time goes in v2:
time: 168 us; the launch traced here: 167 us
  Pallas kernels  162 us (96%)
  local copies, waits for them, and re-layouts  3.62 us (2%)
    pallas_call x1, Pallas kernels, shards(): pl.pallas_call(functools.partial(kernel, devices, 1.0 / math.sqrt(dim)),...  162 us
    unnamed x4, local copies, waits for them, and re-layouts  3.62 us

profile of v2, /device:TPU:18, one launch (start us, length us, event | category | flops | bytes accessed | tf_op | source)
XLA Modules:
  0.0 166.7 jit_solution(13453879136551889478)
XLA Ops:
  0.6 162.5 %shard_map.95 = (bf16[128,5120]{1,0:T(8,128)(2,1)}, bf16[128,5120]{1,0:T(8,128)(2,1)}) custom-call(s32[40]{0:T(128)} %band_ref.1, bf16[128,5120]{1,0:T(8,128)(2,1)} %query_ref.1, bf16[128,5120]{1,0:T(8,128)(2,1)} %key_ref.1, bf16[128,5120]{1,0:T(8,128)(2,1)} %value_ref.1, bf16[128,5120]{1,0:T(8,128)(2,1)} %cross_ref.1, bf16[256,4096]{1,0:T(8,128)(2,1)} %context_ref.1, ...), custom_call_target="tpu_custom_call" | custom-call | flops 6442450944 | bytes 10485760 | tf_op jit(solution)/shard_map/pallas_call | solution.py:369
  163.1 0.0 copy-start
  163.1 2.6 %copy.12 = bf16[128,5120]{1,0:T(8,128)(2,1)} copy(bf16[128,5120]{1,0:T(8,128)(2,1)} %get-tuple-element.4) | data formatting | bytes 2621440
  165.7 0.0 copy-done
  165.7 1.1 copy.13
Async XLA Ops:
  163.1 2.6 %copy-start = (bf16[128,5120]{1,0:T(8,128)(2,1)S(1)}, bf16[128,5120]{1,0:T(8,128)(2,1)}, u32[]{:S(2)}) copy-start(bf16[128,5120]{1,0:T(8,128)(2,1)} %get-tuple-element.5) | copy-start | bytes 3932164

commit v3 on v2

--- a/solution.py
+++ b/solution.py
@@ -42,6 +42,10 @@
     text_recv_sem,
     pass_send_sem,
     pass_recv_sem,
+    scores,
+    weights,
+    totals,
+    summed,
 ):
     heads = band_ref.shape[0]
     rows = query_ref.shape[0]
@@ -238,35 +242,58 @@
         pltpu.make_async_copy(whole, whole, sem).wait()
 
     stripe_len = held.shape[2]
-    tile = 2 * rows
+    tile = scores.shape[1]
+    tiles = stripe_len // tile
 
     def attend(slot, head):
         band = band_ref[head]
         block_ids = lax.broadcasted_iota(jnp.int32, (1, stripe_len), 1) // rows
 
-        def attend_tile(step, carry):
-            at = pl.ds(pl.multiple_of(step * tile, tile), tile)
-            scores = lax.dot_general(
-                held[slot, 0, at, :], held[slot, 1], NT, preferred_element_type=jnp.float32
-            )
-            for half in range(2):
-                gap = jnp.abs(block_ids - (2 * step + half))
-                mask = jnp.where(gap <= band, 0.0, -jnp.inf)
-                part = scores[half * rows : (half + 1) * rows] + mask
-                top = jnp.max(part, axis=1, keepdims=True)
-                weights = jnp.exp2((part - top) * (scale * math.log2(math.e)))
-                total = jnp.sum(weights, axis=1, keepdims=True)
-                summed = jnp.dot(
-                    weights.astype(jnp.bfloat16),
-                    held[slot, 2],
-                    preferred_element_type=jnp.float32,
-                )
-                attended[slot, block_rows(2 * step + half), :] = (summed / total).astype(
-                    jnp.bfloat16
-                )
-            return carry
-
-        lax.fori_loop(0, stripe_len // tile, attend_tile, 0)
+        def score(step, part):
+            cols = pl.ds(pl.multiple_of(part * tile, tile), tile)
+            scores[step % 2, :, cols] = lax.dot_general(
+                held[slot, 0, step * tile : (step + 1) * tile, :],
+                held[slot, 1, cols, :],
+                NT,
+                preferred_element_type=jnp.float32,
+            )
+
+        def weigh(step, part):
+            gap = jnp.abs(block_ids - (step * (tile // rows) + part))
+            mask = jnp.where(gap <= band, 0.0, -jnp.inf)
+            masked = scores[step % 2, block_rows(part), :] + mask
+            top = jnp.max(masked, axis=1, keepdims=True)
+            raised = jnp.exp2((masked - top) * (scale * math.log2(math.e)))
+            total = jnp.sum(raised, axis=1, keepdims=True)
+            totals[step % 2, block_rows(part), :] = jnp.broadcast_to(total, (rows, dim))
+            weights[step % 2, block_rows(part), :] = raised.astype(jnp.bfloat16)
+
+        def add_up(step, part):
+            cols = pl.ds(pl.multiple_of(part * tile, tile), tile)
+            summed[...] += jnp.dot(
+                weights[step % 2, :, cols],
+                held[slot, 2, cols, :],
+                preferred_element_type=jnp.float32,
+            )
+
+        for step in range(-1, tiles + 1):
+
+            def stage(part, carry, step=step):
+                if step + 1 < tiles:
+                    score(step + 1, part)
+                if 0 <= step < tiles:
+                    weigh(step, part)
+                if step >= 1:
+                    add_up(step - 1, part)
+                return carry
+
+            if step >= 1:
+                summed[...] = jnp.zeros_like(summed)
+            lax.fori_loop(0, stripe_len // tile, stage, 0)
+            if step >= 1:
+                attended[slot, (step - 1) * tile : step * tile, :] = (
+                    summed[...] / totals[(step - 1) % 2]
+                ).astype(jnp.bfloat16)
 
     def give_back(slot, head):
         def give(step, carry):
@@ -294,16 +321,14 @@
     def cross():
         def cross_head(head, carry):
             at = pl.ds(pl.multiple_of(head * dim, dim), dim)
-            scores = jnp.dot(
-                cross_ref[:, at], text[0, at, :], preferred_element_type=jnp.float32
-            )
-            top = jnp.max(scores, axis=1, keepdims=True)
-            weights = jnp.exp2((scores - top) * (scale * math.log2(math.e)))
-            total = jnp.sum(weights, axis=1, keepdims=True)
-            summed = lax.dot_general(
-                weights.astype(jnp.bfloat16), text[1, at, :], NT, preferred_element_type=jnp.float32
-            )
-            cross_out_ref[:, at] = (summed / total).astype(jnp.bfloat16)
+            part = jnp.dot(cross_ref[:, at], text[0, at, :], preferred_element_type=jnp.float32)
+            top = jnp.max(part, axis=1, keepdims=True)
+            raised = jnp.exp2((part - top) * (scale * math.log2(math.e)))
+            total = jnp.sum(raised, axis=1, keepdims=True)
+            mixed = lax.dot_general(
+                raised.astype(jnp.bfloat16), text[1, at, :], NT, preferred_element_type=jnp.float32
+            )
+            cross_out_ref[:, at] = (mixed / total).astype(jnp.bfloat16)
             return carry
 
         lax.fori_loop(0, heads, cross_head, 0, unroll=4 if heads % 4 == 0 else 1)
@@ -399,6 +424,10 @@
             pltpu.SemaphoreType.DMA((2,)),
             pltpu.SemaphoreType.DMA((2, devices // PLANE)),
             pltpu.SemaphoreType.DMA((2, devices // PLANE)),
+            pltpu.VMEM((2, PLANE * rows, SB * rows), jnp.float32),
+            pltpu.VMEM((2, PLANE * rows, SB * rows), dtype),
+            pltpu.VMEM((2, PLANE * rows, dim), jnp.float32),
+            pltpu.VMEM((PLANE * rows, dim), jnp.float32),
         ],
         compiler_params=pltpu.CompilerParams(
             collective_id=0, has_side_effects=True, vmem_limit_bytes=56 * 1024 * 1024

time: 168 us -> 177 us (1.054)
  Pallas kernels: 162 us -> 172 us
    pallas_call x1, Pallas kernels: 162 us -> 172 us  [shards(): pl.pallas_call(functools.partial(kernel, devices, 1.0 / math.sqrt(dim)),...]
where the time goes in v3:
time: 177 us; the launch traced here: 176 us
  Pallas kernels  172 us (97%)
  local copies, waits for them, and re-layouts  3.62 us (2%)
    pallas_call x1, Pallas kernels, shards(): pl.pallas_call(functools.partial(kernel, devices, 1.0 / math.sqrt(dim)),...  172 us
    unnamed x4, local copies, waits for them, and re-layouts  3.62 us

profile of v3, /device:TPU:18, one launch (start us, length us, event | category | flops | bytes accessed | tf_op | source)
XLA Modules:
  0.0 176.1 jit_solution(16881243624780500657)
XLA Ops:
  0.6 171.8 %shard_map.95 = (bf16[128,5120]{1,0:T(8,128)(2,1)}, bf16[128,5120]{1,0:T(8,128)(2,1)}) custom-call(s32[40]{0:T(128)} %band_ref.1, bf16[128,5120]{1,0:T(8,128)(2,1)} %query_ref.1, bf16[128,5120]{1,0:T(8,128)(2,1)} %key_ref.1, bf16[128,5120]{1,0:T(8,128)(2,1)} %value_ref.1, bf16[128,5120]{1,0:T(8,128)(2,1)} %cross_ref.1, bf16[256,4096]{1,0:T(8,128)(2,1)} %context_ref.1, ...), custom_call_target="tpu_custom_call" | custom-call | flops 6442450944 | bytes 10485760 | tf_op jit(solution)/shard_map/pallas_call | solution.py:394
  172.5 0.0 copy-start
  172.5 2.6 %copy.12 = bf16[128,5120]{1,0:T(8,128)(2,1)} copy(bf16[128,5120]{1,0:T(8,128)(2,1)} %get-tuple-element.4) | data formatting | bytes 2621440
  175.0 0.0 copy-done
  175.0 1.1 copy.13
Async XLA Ops:
  172.5 2.6 %copy-start = (bf16[128,5120]{1,0:T(8,128)(2,1)S(1)}, bf16[128,5120]{1,0:T(8,128)(2,1)}, u32[]{:S(2)}) copy-start(bf16[128,5120]{1,0:T(8,128)(2,1)} %get-tuple-element.5) | copy-start | bytes 3932164

commit v4 on v2

--- a/solution.py
+++ b/solution.py
@@ -164,6 +164,26 @@
             pltpu.make_async_copy(piece, piece, pass_recv_sem.at[(side + 1) // 2, hop]).wait()
 
     cuts = [1 + (SB - 1) * part // planes for part in range(planes + 1)]
+    if rest:
+        mine = (me % stride == 0) & (me // stride < rest)
+        base = me // stride
+
+        def send_rest(step, carry):
+            index = (base + step) % rest
+            send_head(full, full * SB + index, index * stride, send_sem.at[full])
+            return carry
+
+        lax.fori_loop(1, rest, send_rest, 0)
+        first = base % rest
+
+        @pl.when(mine)
+        def _():
+            keep_head(full, full * SB + first)
+
+        @pl.when(jnp.logical_not(mine))
+        def _():
+            send_head(full, full * SB + first, first * stride, edge_sem)
+
     send_full(0, cuts[0], cuts[1])
     keep_head(0, me)
     for load in loads:
@@ -195,26 +215,6 @@
     for slot in range(1, full):
         send_full(slot, 1, SB)
         keep_head(slot, slot * SB + me)
-
-    if rest:
-        mine = (me % stride == 0) & (me // stride < rest)
-        base = me // stride
-
-        def send_rest(step, carry):
-            index = (base + step) % rest
-            send_head(full, full * SB + index, index * stride, send_sem.at[full])
-            return carry
-
-        lax.fori_loop(1, rest, send_rest, 0)
-        first = base % rest
-
-        @pl.when(mine)
-        def _():
-            keep_head(full, full * SB + first)
-
-        @pl.when(jnp.logical_not(mine))
-        def _():
-            send_head(full, full * SB + first, first * stride, edge_sem)
 
     def forward_text(phase, peer, places):
         for at in places:
@@ -311,24 +311,29 @@
     for side in (-1, 1):
         take_text(planes - 2, side)
     forward_text(0, across, (place,))
+    if rest:
+
+        @pl.when(mine)
+        def _():
+            wait_held(full)
+            attend(full, full * SB + first)
+            give_back(full, full * SB + first)
+
+    wait_text(text_recv_sem.at[0], planes)
+    forward_text(1, beside, (place, (1 - place // 2) * 2 + place % 2))
     wait_held(0)
     attend(0, me)
     give_back(0, me)
-    wait_text(text_recv_sem.at[0], planes)
-    forward_text(1, beside, (place, (1 - place // 2) * 2 + place % 2))
+    wait_text(text_recv_sem.at[1], 2 * planes)
+    cross()
     for slot in range(1, full):
         wait_held(slot)
         attend(slot, slot * SB + me)
         give_back(slot, slot * SB + me)
-    wait_text(text_recv_sem.at[1], 2 * planes)
-    cross()
     if rest:
 
         @pl.when(mine)
         def _():
-            wait_held(full)
-            attend(full, full * SB + first)
-            give_back(full, full * SB + first)
             done = attended.at[full, pl.ds(0, (SB - 1) * rows), :]
             pltpu.make_async_copy(done, done, back_send_sem.at[full]).wait()
 

time: 168 us -> 173 us (1.030); the launches traced: 167 us -> 169 us
  Pallas kernels: 162 us -> 165 us
    pallas_call x1, Pallas kernels: 162 us -> 165 us  [shards(): pl.pallas_call(functools.partial(kernel, devices, 1.0 / math.sqrt(dim)),...]
where the time goes in v4:
time: 173 us; the launch traced here: 169 us
  Pallas kernels  165 us (95%)
  local copies, waits for them, and re-layouts  3.62 us (2%)
    pallas_call x1, Pallas kernels, shards(): pl.pallas_call(functools.partial(kernel, devices, 1.0 / math.sqrt(dim)),...  165 us
    unnamed x4, local copies, waits for them, and re-layouts  3.62 us

profile of v4, /device:TPU:18, one launch (start us, length us, event | category | flops | bytes accessed | tf_op | source)
XLA Modules:
  0.0 169.2 jit_solution(9354008203863214275)
XLA Ops:
  0.6 164.9 %shard_map.95 = (bf16[128,5120]{1,0:T(8,128)(2,1)}, bf16[128,5120]{1,0:T(8,128)(2,1)}) custom-call(s32[40]{0:T(128)} %band_ref.1, bf16[128,5120]{1,0:T(8,128)(2,1)} %query_ref.1, bf16[128,5120]{1,0:T(8,128)(2,1)} %key_ref.1, bf16[128,5120]{1,0:T(8,128)(2,1)} %value_ref.1, bf16[128,5120]{1,0:T(8,128)(2,1)} %cross_ref.1, bf16[256,4096]{1,0:T(8,128)(2,1)} %context_ref.1, ...), custom_call_target="tpu_custom_call" | custom-call | flops 6442450944 | bytes 10485760 | tf_op jit(solution)/shard_map/pallas_call | solution.py:374
  165.6 0.0 copy-start
  165.6 2.6 %copy.12 = bf16[128,5120]{1,0:T(8,128)(2,1)} copy(bf16[128,5120]{1,0:T(8,128)(2,1)} %get-tuple-element.4) | data formatting | bytes 2621440
  168.1 0.0 copy-done
  168.1 1.1 copy.13
Async XLA Ops:
  165.6 2.6 %copy-start = (bf16[128,5120]{1,0:T(8,128)(2,1)S(1)}, bf16[128,5120]{1,0:T(8,128)(2,1)}, u32[]{:S(2)}) copy-start(bf16[128,5120]{1,0:T(8,128)(2,1)} %get-tuple-element.5) | copy-start | bytes 3932164
